TPU v7x, 32 devices: a whole 2x2x4 slice. The times are simulated.
32 devices in a mesh: node: 16 (over z, x, core), local: 2 (over y).
Axes of the slice: x: 2, y: 2, z: 4, core: 2. Of those that a mesh axis runs over, the one named last changes fastest.
Arguments:
- tokens: bfloat16 [256, 4096], P('node', 'local'), may hold values from -6 to 6
- grad_out: bfloat16 [256, 4096], P('node', 'local'), may hold values from -6 to 6
- gates: float32 [256, 8], P('node'), may hold values from 0.1 to 1
- expert_ids: int32 [256, 8], P('node'), may hold values from 0 to 15, all different within a row; in each aligned block of 16 rows (0 to 15, 16 to 31, ...) at most 16 rows name the same one
- w_gate: bfloat16 [16, 4096, 1024], P('node', 'local'), may hold values from -0.09375 to 0.09375
- w_up: bfloat16 [16, 4096, 1024], P('node', 'local'), may hold values from -0.09375 to 0.09375
- w_down: bfloat16 [16, 1024, 4096], P('node', None, 'local'), may hold values from -0.046875 to 0.046875
Outputs:
- grad_tokens: bfloat16 [256, 4096], P('node', 'local')
- grad_gates: bfloat16 [256, 8], P('node')
Inputs may be any that keep to these rules, and one draw needn't show every extreme that they name: `expert_ids`: each row names 8 different experts. Among the 16 rows of one node rank no expert is named by more than 16 rows, a bound that some block reaches.
All inputs are finite; a program needn't handle non-finite values.
Results may differ from a plain program's by a relative error of at most 0.0057.
Values may be sent and summed in bfloat16 or wider, within the bound.
A program may use at most 64 MiB of HBM per device.

v0:
```python
import jax
import jax.numpy as jnp
from jax import lax
from jax.sharding import PartitionSpec as P


def local_grads(gate_pre, up_pre, back_pre, reduce_axis):
    sigmoid_gate = jax.nn.sigmoid(gate_pre)
    act = gate_pre * sigmoid_gate
    partial_gate = jnp.sum(act * up_pre * back_pre, axis=reduce_axis)
    grad_up = (back_pre * act).astype(jnp.bfloat16)
    grad_gate = (back_pre * up_pre * sigmoid_gate * (1.0 + gate_pre * (1.0 - sigmoid_gate))).astype(
        jnp.bfloat16
    )
    return (grad_gate, grad_up, partial_gate)


def on_device(tokens, grad_out, gates, expert_ids, w_gate, w_up, w_down):
    n_node = lax.axis_size("node")
    tok_rows, feature_cols = tokens.shape
    top_count = expert_ids.shape[1]
    capacity = min(tok_rows, max(2, 2 * tok_rows * top_count // n_node))
    flat_ids = expert_ids.reshape(-1)
    onehot = (flat_ids[:, None] == jnp.arange(n_node, dtype=jnp.int32)[None, :]).astype(jnp.int32)
    slot_rank = jnp.sum(onehot * (jnp.cumsum(onehot, axis=0) - 1), axis=1)
    target = flat_ids * capacity + slot_rank
    placed = (target[:, None] == jnp.arange(n_node * capacity, dtype=jnp.int32)[None, :]).astype(
        jnp.bfloat16
    )
    paired = jnp.repeat(jnp.concatenate([tokens, grad_out], axis=1), top_count, axis=0)
    outgoing = lax.dot_general(
        placed, paired, (((0,), (0,)), ((), ())), preferred_element_type=jnp.float32
    )
    outgoing = outgoing.astype(jnp.bfloat16).reshape(n_node, capacity, 2 * feature_cols)
    gate_cols = w_gate[0]
    up_cols = w_up[0]
    down_rows = w_down[0]
    incoming = lax.all_to_all(outgoing, "node", split_axis=0, concat_axis=0, tiled=True)
    sources = incoming.shape[0]
    slot_count = incoming.shape[1]
    row_count = sources * slot_count
    flat_in = incoming.reshape(row_count, 2 * feature_cols)
    x_rows = flat_in[:, :feature_cols]
    dy_rows = flat_in[:, feature_cols:]
    gate_pre = lax.dot_general(
        gate_cols, x_rows, (((0,), (1,)), ((), ())), preferred_element_type=jnp.float32
    )
    up_pre = lax.dot_general(
        up_cols, x_rows, (((0,), (1,)), ((), ())), preferred_element_type=jnp.float32
    )
    back_pre = lax.dot_general(
        down_rows, dy_rows, (((1,), (1,)), ((), ())), preferred_element_type=jnp.float32
    )
    summed = lax.psum_scatter(
        jnp.concatenate([gate_pre, up_pre, back_pre], axis=1),
        "local",
        scatter_dimension=0,
        tiled=True,
    )
    grad_gate, grad_up, partial_gate = local_grads(
        summed[:, :row_count], summed[:, row_count : 2 * row_count], summed[:, 2 * row_count :], 0
    )
    running = lax.dot_general(
        lax.all_gather(grad_gate, "local", axis=0, tiled=True),
        gate_cols,
        (((0,), (1,)), ((), ())),
        preferred_element_type=jnp.float32,
    )
    result = running + lax.dot_general(
        lax.all_gather(grad_up, "local", axis=0, tiled=True),
        up_cols,
        (((0,), (1,)), ((), ())),
        preferred_element_type=jnp.float32,
    )
    gate_total = lax.psum(partial_gate, "local").astype(jnp.bfloat16)
    sent_rows = result.astype(jnp.bfloat16).reshape(sources, slot_count, feature_cols)
    sent_gates = gate_total.reshape(sources, slot_count)
    back_rows = lax.all_to_all(sent_rows, "node", split_axis=0, concat_axis=0, tiled=True)
    back_gates = lax.all_to_all(sent_gates, "node", split_axis=0, concat_axis=0, tiled=True)
    picked = jnp.take(back_rows.reshape(n_node * capacity, feature_cols), target, axis=0)
    picked = picked.reshape(tok_rows, top_count, feature_cols).astype(jnp.float32)
    grad_tokens = jnp.sum(picked * gates[:, :, None], axis=1).astype(jnp.bfloat16)
    grad_gates = jnp.take(back_gates.reshape(-1), target, axis=0).reshape(tok_rows, top_count)
    return (grad_tokens, grad_gates)


def solution(mesh):
    in_specs = (
        P("node", "local"),
        P("node", "local"),
        P("node", None),
        P("node", None),
        P("node", "local", None),
        P("node", "local", None),
        P("node", None, "local"),
    )
    out_specs = (P("node", "local"), P("node", None))
    return jax.shard_map(
        on_device, mesh=mesh, in_specs=in_specs, out_specs=out_specs, check_vma=False
    )
```

profile of v0, /device:TPU:0, one launch (start us, length us, event | category | flops | bytes accessed | tf_op | source)
XLA Modules:
  0.0 192.6 jit_solution(6725815519121996547)
XLA Ops:
  7.2 0.0 reduce-scatter.2.cloned.1.call-start
  7.2 0.8 copy.17
  8.0 0.1 reshape.82
  8.1 0.1 fusion.32
  8.2 0.2 reduce_window_sum.11
  8.3 0.2 select_reduce_fusion
  8.5 0.9 pad_maximum_fusion.1
  9.4 0.0 copy-start.3
  9.4 0.8 convolution_convert_fusion
  10.2 54.6 %all_to_all.20 = bf16[16,16,4096]{2,1,0:T(8,128)(2,1)S(1)} all-to-all(bf16[16,16,4096]{2,1,0:T(8,128)(2,1)S(1)} %bitcast.49), channel_id=1, replica_groups=mesh['node'=16,'local'=2] {'node'}, dimensions={0} | all-to-all | bytes 4194304 | tf_op jit(solution)/shard_map/all_to_all | solution.py:38
  64.8 0.0 copy-done.3
  64.8 0.0 copy-start.2
  64.8 1.3 fusion.16
  66.1 0.9 copy-done.2
  67.0 0.0 copy-start.1
  67.0 1.3 fusion.19
  68.3 0.9 copy-done.1
  69.2 1.4 fusion.22
  70.6 2.1 %pad_maximum_fusion = f32[1024,768]{0,1:T(8,128)} fusion(f32[1024,256]{0,1:T(8,128)S(1)} %fusion.22, f32[1024,256]{0,1:T(8,128)S(1)} %fusion.19, f32[1024,256]{0,1:T(8,128)S(1)} %fusion.16), kind=kLoop, calls=%fused_computation.13 | loop fusion | flops 1572864 | bytes 6291456 | tf_op jit(solution)/shard_map/concatenate | solution.py:55
  72.7 0.0 reduce-scatter.2.cloned.1.call-update
  72.7 44.0 %reduce-scatter.2.cloned.1.call-done = f32[512,768]{0,1:T(8,128)} async-done(((f32[1024,768]{0,1:T(8,128)}), f32[512,768]{0,1:T(8,128)}) %reduce-scatter.2.cloned.1.call-update) | async-done | bytes 1572880 | tf_op jit(solution)/shard_map/reduce_scatter | solution.py:54
  116.7 1.7 multiply_reduce_fusion.1
  118.4 8.7 %all_gather.7 = bf16[1024,256]{0,1:T(8,128)(2,1)S(1)} all-gather(bf16[512,256]{0,1:T(8,128)(2,1)S(1)} %get-tuple-element.12), channel_id=1, replica_groups=mesh['node'=16,'local'=2] {'local'}, dimensions={0}, use_global_device_ids=true | all-gather | bytes 786432 | tf_op jit(solution)/shard_map/all_gather | solution.py:70
  127.1 3.5 %fusion.2 = f32[256,2048]{1,0:T(8,128)S(1)} fusion(bf16[1024,256]{0,1:T(8,128)(2,1)S(1)} %all_gather.7, bf16[1,2048,1024]{2,1,0:T(8,128)(2,1)} %param.12), kind=kOutput, calls=%fused_computation.5 | convolution fusion | flops 1073741824 | bytes 6815744 | tf_op jit(solution)/shard_map/dot_general | solution.py:69
  130.6 7.8 %all_gather.6 = bf16[1024,256]{0,1:T(8,128)(2,1)S(1)} all-gather(bf16[512,256]{0,1:T(8,128)(2,1)S(1)} %get-tuple-element.11), channel_id=1, replica_groups=mesh['node'=16,'local'=2] {'local'}, dimensions={0}, use_global_device_ids=true | all-gather | bytes 786432 | tf_op jit(solution)/shard_map/all_gather | solution.py:64
  138.4 4.9 %psum.7 = bf16[256]{0:T(256)(128)(2,1)S(1)} all-reduce(f32[256]{0:T(256)S(1)} %get-tuple-element.10), channel_id=1, replica_groups=mesh['node'=16,'local'=2] {'local'}, use_global_device_ids=true, to_apply=%region_5.6 | all-reduce | flops 256 | bytes 1536 | tf_op jit(solution)/shard_map/psum | solution.py:75
  143.4 0.7 all_to_all.16
  144.1 5.7 %all-to-all-start.2 = ((bf16[16,1,16]{2,1,0:T(2,128)(2,1)}), bf16[16,1,16]{2,1,0:T(2,128)(2,1)S(1)}, u32[]{:S(2)}, u32[]{:S(2)}) async-start(bf16[16,1,16]{2,1,0:T(2,128)(2,1)} %all_to_all.16), calls=%async_computation.3 | async-start | bytes 16384 | tf_op jit(solution)/shard_map/all_to_all | solution.py:79
  149.7 0.0 copy-start
  149.8 4.5 %fusion.13 = bf16[256,2048]{1,0:T(8,128)(2,1)} fusion(f32[256,2048]{1,0:T(8,128)S(1)} %fusion.2, bf16[1024,256]{0,1:T(8,128)(2,1)S(1)} %all_gather.6, bf16[1,2048,1024]{2,1,0:T(8,128)(2,1)} %param.11), kind=kOutput, calls=%fused_computation.15 | convolution fusion | flops 1074790400 | bytes 7864320 | tf_op jit(solution)/shard_map/dot_general | solution.py:63
  154.3 1.8 all-to-all-done.2
  156.1 4.2 %all-to-all-start.1 = ((bf16[16,16,2048]{2,1,0:T(8,128)(2,1)}), bf16[16,16,2048]{2,1,0:T(8,128)(2,1)S(1)}, u32[]{:S(2)}, u32[]{:S(2)}) async-start(bf16[16,16,2048]{2,1,0:T(8,128)(2,1)} %bitcast.9), calls=%async_computation.2 | async-start | bytes 2097152 | tf_op jit(solution)/shard_map/all_to_all | solution.py:78
  160.3 0.1 reduce_sum.32
  160.4 0.1 mul.73
  160.5 0.0 copy-done
  160.5 0.1 copy.19
  160.6 0.1 reshape.88
  160.7 1.2 gather_fusion.1
  161.9 0.1 gather.15
  162.1 0.7 copy.21
  162.7 20.5 %all-to-all-done.1 = bf16[16,16,2048]{2,1,0:T(8,128)(2,1)S(1)} async-done(((bf16[16,16,2048]{2,1,0:T(8,128)(2,1)}), bf16[16,16,2048]{2,1,0:T(8,128)(2,1)S(1)}, u32[]{:S(2)}, u32[]{:S(2)}) %all-to-all-start.1) | async-done | bytes 1048608 | tf_op jit(solution)/shard_map/all_to_all | solution.py:78
  183.2 0.9 gather_fusion
  184.2 1.6 multiply_reduce_fusion
  (6 shorter events, 0.1 us)
Async XLA Ops:
  7.2 109.5 %reduce-scatter.2.cloned.1.call-start = ((), (), s32[]{:S(2)}) async-start(), calls=%async_computation.4 | async-start | bytes 4718592 | tf_op jit(solution)/shard_map/reduce_scatter | solution.py:54
  9.4 55.4 %copy-start.3 = (bf16[1,2048,1024]{2,1,0:T(8,128)(2,1)S(1)}, bf16[1,2048,1024]{2,1,0:T(8,128)(2,1)}, u32[]{:S(2)}) copy-start(bf16[1,2048,1024]{2,1,0:T(8,128)(2,1)} %param.11) | copy-start | bytes 12582916
  64.8 2.2 %copy-start.2 = (bf16[1,2048,1024]{2,1,0:T(8,128)(2,1)S(1)}, bf16[1,2048,1024]{2,1,0:T(8,128)(2,1)}, u32[]{:S(2)}) copy-start(bf16[1,2048,1024]{2,1,0:T(8,128)(2,1)} %param.12) | copy-start | bytes 12582916
  67.0 2.2 %copy-start.1 = (bf16[1,1024,2048]{2,1,0:T(8,128)(2,1)S(1)}, bf16[1,1024,2048]{2,1,0:T(8,128)(2,1)}, u32[]{:S(2)}) copy-start(bf16[1,1024,2048]{2,1,0:T(8,128)(2,1)} %param.13) | copy-start | bytes 12582916
  144.1 12.0 %all-to-all-start.2 = ((bf16[16,1,16]{2,1,0:T(2,128)(2,1)}), bf16[16,1,16]{2,1,0:T(2,128)(2,1)S(1)}, u32[]{:S(2)}, u32[]{:S(2)}) async-start(bf16[16,1,16]{2,1,0:T(2,128)(2,1)} %all_to_all.16), calls=%async_computation.3 | async-start | bytes 16384 | tf_op jit(solution)/shard_map/all_to_all | solution.py:79
  149.7 10.7 %copy-start = (f32[16,8]{0,1:T(8,128)S(1)}, f32[16,8]{0,1:T(8,128)}, u32[]{:S(2)}) copy-start(f32[16,8]{0,1:T(8,128)} %param.9) | copy-start | bytes 1540
  156.1 27.2 %all-to-all-start.1 = ((bf16[16,16,2048]{2,1,0:T(8,128)(2,1)}), bf16[16,16,2048]{2,1,0:T(8,128)(2,1)S(1)}, u32[]{:S(2)}, u32[]{:S(2)}) async-start(bf16[16,16,2048]{2,1,0:T(8,128)(2,1)} %bitcast.9), calls=%async_computation.2 | async-start | bytes 2097152 | tf_op jit(solution)/shard_map/all_to_all | solution.py:78
Sparse Core Ops, SparseCore 0:
  72.9 43.7 reduce-scatter.1
where the time goes:
time: 194 us; the launch traced here: 193 us
  blocking collectives  76.1 us (39%)
  waiting for transfers between devices  66.3 us (34%)
  between operations  14.2 us (7%)
  matrix products  12.8 us (7%)
  starting transfers between devices  9.93 us (5%)
  other arithmetic  6.78 us (3%)
  local copies, waits for them, and re-layouts  6.59 us (3%)
    all_to_all x1, blocking collectives, on_device(): lax.all_to_all(outgoing, 'node', split_axis=0, concat_axis=0, tiled=True)  54.6 us
    reduce_scatter x1, waiting for transfers between devices, on_device(): lax.psum_scatter(jnp.concatenate([gate_pre, up_pre, back_pre], axis=1), '...  44 us
    all_to_all x1, waiting for transfers between devices, on_device(): lax.all_to_all(sent_rows, 'node', split_axis=0, concat_axis=0, tiled=True)  20.5 us
    all_gather x1, blocking collectives, on_device(): lax.all_gather(grad_up, 'local', axis=0, tiled=True)  8.7 us
    all_gather x1, blocking collectives, on_device(): lax.all_gather(grad_gate, 'local', axis=0, tiled=True)  7.82 us
    all_to_all x1, starting transfers between devices, on_device(): lax.all_to_all(sent_gates, 'node', split_axis=0, concat_axis=0, tiled=True)  5.69 us
    psum x1, blocking collectives, on_device(): gate_total = lax.psum(partial_gate, 'local').astype(jnp.bfloat16)  4.92 us
    dot_general x1, matrix products, on_device(): lax.dot_general(lax.all_gather(grad_gate, 'local', axis=0, tiled=True), g...  4.51 us
  transfers between devices with their start and end apart: 3, of which 3 were waited for; matrix products, arithmetic and copies ran while one was open for 4% of the time, Pallas kernels for 0%

commit v1 on v0

--- a/solution.py
+++ b/solution.py
@@ -1,7 +1,258 @@
+import functools
+
 import jax
 import jax.numpy as jnp
 from jax import lax
+from jax.experimental import pallas as pl
+from jax.experimental.pallas import tpu as pltpu
 from jax.sharding import PartitionSpec as P
+
+MESH = pl.DeviceIdType.MESH
+LANES = 128
+TILE = 256
+AG_Z, AG_X, AG_A, AG_B, SUM_Y, GRAD_Y, RS_C, RS_X, RS_Z, KINDS = 0, 1, 2, 3, 4, 7, 8, 9, 10, 11
+NT = (((1,), (1,)), ((), ()))
+
+
+def flipped(value, bits):
+    place = 1
+    while place <= bits:
+        if bits & place:
+            value = value + place * (1 - 2 * lax.rem(lax.div(value, place), 2))
+        place *= 2
+    return value
+
+
+def dense_kernel(
+    planes, tokens, grad_out, gates, ids, wg_hbm, wu_hbm, wd_hbm, out, out_gates,
+    wg, wu, wd, gath, part, sum_send, sum_recv, grads, pair, rc_send, rc_recv,
+    rx_send, rx_recv, rz_send, rz_recv, w_sem, send_sem, recv_sem,
+):
+    node, y = lax.axis_index("node"), lax.axis_index("local")
+    core, x, z = lax.rem(node, 2), lax.rem(lax.div(node, 2), 2), lax.div(node, 4)
+    rows, feat = tokens.shape
+    hidden = wg.shape[1]
+    experts = 4 * planes
+    half = 2 * rows
+    f32, bf16 = jnp.float32, jnp.bfloat16
+
+    def device(z_, x_, c_):
+        return (z_ * 4 + x_ * 2 + c_, y)
+
+    x_peer, sibling = device(z, 1 - x, core), device(z, x, 1 - core)
+    y_peer = (node, 1 - y)
+    z_peers = [None] + [device(flipped(z, k), x, core) for k in range(1, planes)]
+
+    def block(x_, c_, size=rows):
+        return pl.ds(pl.multiple_of((x_ * 2 + c_) * rows, rows), size)
+
+    mine, here = block(x, core), block(y, 0, half)
+    theirs = block(1 - y, 0, half)
+
+    loads = [
+        pltpu.make_async_copy(src.at[0], dst, w_sem.at[i])
+        for i, (src, dst) in enumerate(((wg_hbm, wg), (wu_hbm, wu), (wd_hbm, wd)))
+    ]
+    for load in loads:
+        load.start()
+
+    barrier = pltpu.get_barrier_semaphore()
+    peers = [x_peer, sibling, y_peer] + z_peers[1:]
+    for peer in peers:
+        pl.semaphore_signal(barrier, inc=1, device_id=peer, device_id_type=MESH)
+
+    gath[0, mine, :feat] = tokens[...]
+    gath[0, mine, feat : 2 * feat] = grad_out[...]
+    lane = lax.broadcasted_iota(jnp.int32, (rows, LANES), 1)
+    expert_lane = lax.rem(lane, experts)
+    weight = jnp.zeros((rows, LANES), f32)
+    for j in range(ids.shape[1]):
+        weight = weight + jnp.where(expert_lane == ids[:, j : j + 1], gates[:, j : j + 1], 0.0)
+    top = weight.astype(bf16).astype(f32)
+    middle = (weight - top).astype(bf16).astype(f32)
+    low = weight - top - middle
+    packed = jnp.where(
+        lane < experts, top, jnp.where(lane < 2 * experts, middle, jnp.where(lane < 3 * experts, low, 0.0))
+    )
+    gath[0, mine, 2 * feat :] = packed.astype(bf16)
+
+    pl.semaphore_wait(barrier, len(peers))
+
+    copies = {}
+
+    def send(kind, k, src, dst, peer):
+        copies[kind, k] = pltpu.make_async_remote_copy(
+            src_ref=src, dst_ref=dst, send_sem=send_sem.at[k, kind], recv_sem=recv_sem.at[k, kind],
+            device_id=peer, device_id_type=MESH,
+        )
+        copies[kind, k].start()
+
+    def arrived(kind, k):
+        copies[kind, k].wait_recv()
+
+    def forward(kind, k, where, peer):
+        send(kind, k, gath.at[k, where], gath.at[k, where], peer)
+
+    def gather_column(k):
+        if k:
+            arrived(AG_Z, k)
+        forward(AG_X, k, mine, x_peer)
+        if k == 0:
+            for far in range(1, planes):
+                send(AG_Z, far, gath.at[0, mine], gath.at[far, mine], z_peers[far])
+        forward(AG_A, k, mine, sibling)
+
+    def gather_plane(k):
+        arrived(AG_X, k)
+        forward(AG_B, k, block(1 - x, core), sibling)
+
+    def first_products(k):
+        arrived(AG_A, k)
+        arrived(AG_B, k)
+        for m in range(3):
+            if k == 0:
+                loads[m].wait()
+
+            def column_tile(j, carry, m=m):
+                at = pl.ds(pl.multiple_of(j * TILE, TILE), TILE)
+                if m < 2:
+                    value = jnp.dot(gath[k, :, :feat], (wg, wu)[m][:, at], preferred_element_type=f32)
+                else:
+                    value = lax.dot_general(
+                        gath[k, :, feat : 2 * feat], wd[at, :], NT, preferred_element_type=f32
+                    )
+                part[k, m, :, at] = value
+                return carry
+
+            lax.fori_loop(0, hidden // TILE, column_tile, 0)
+            sum_send[k, m] = part[k, m, theirs, :].astype(bf16)
+            send(SUM_Y + m, k, sum_send.at[k, m], sum_recv.at[k, m], y_peer)
+
+    def hidden_grads(k):
+        for m in range(3):
+            arrived(SUM_Y + m, k)
+        total = jnp.zeros((half, 1), f32)
+        for j in range(hidden // TILE):
+            at = pl.ds(j * TILE, TILE)
+            gate, up, back = (
+                part[k, m, here, at] + sum_recv[k, m, :, at].astype(f32) for m in range(3)
+            )
+            sig = jax.nn.sigmoid(gate)
+            act = gate * sig
+            back_act = back * act
+            total = total + jnp.sum(back_act * up, axis=1, keepdims=True)
+            grads[k, here, j * TILE : (j + 1) * TILE] = (
+                back * up * sig * (1.0 + gate * (1.0 - sig))
+            ).astype(bf16)
+            grads[k, here, hidden + j * TILE : hidden + (j + 1) * TILE] = back_act.astype(bf16)
+        lanes = lax.broadcasted_iota(jnp.int32, (half, LANES), 1)
+        grads[k, here, 2 * hidden :] = jnp.where(lanes == node, total, 0.0).astype(bf16)
+        send(GRAD_Y, k, grads.at[k, here], grads.at[k, here], y_peer)
+
+    def second_products(k):
+        arrived(GRAD_Y, k)
+        lanes = lax.broadcasted_iota(jnp.int32, (2 * half, LANES), 1)
+        chosen = (lax.rem(lanes, experts) == node) & (lanes < 3 * experts)
+        scale = jnp.sum(
+            jnp.where(chosen, gath[k, :, 2 * feat :].astype(f32), 0.0), axis=1, keepdims=True
+        )
+
+        def feature_tile(j, carry):
+            at = pl.ds(pl.multiple_of(j * TILE, TILE), TILE)
+            value = lax.dot_general(grads[k, :, :hidden], wg[at, :], NT, preferred_element_type=f32)
+            value = value + lax.dot_general(
+                grads[k, :, hidden : 2 * hidden], wu[at, :], NT, preferred_element_type=f32
+            )
+            pair[k, :, at] = value * scale
+            return carry
+
+        lax.fori_loop(0, feat // TILE, feature_tile, 0)
+        pair[k, :, feat:] = grads[k, :, 2 * hidden :].astype(f32)
+        for x_ in range(2):
+            rc_send[k, x_] = pair[k, block(x_, 1 - core), :].astype(bf16)
+        send(RS_C, k, rc_send.at[k], rc_recv.at[k], sibling)
+
+    def chip_sum(k, x_):
+        return pair[k, block(x_, core), :] + rc_recv[k, x_].astype(f32)
+
+    def reduce_chip(k):
+        arrived(RS_C, k)
+        rx_send[k] = chip_sum(k, 1 - x).astype(bf16)
+        send(RS_X, k, rx_send.at[k], rx_recv.at[k], x_peer)
+
+    def reduce_plane(k):
+        arrived(RS_X, k)
+        value = chip_sum(k, x) + rx_recv[k].astype(f32)
+        if k == 0:
+            pair[0, mine, :] = value
+        else:
+            rz_send[k] = value.astype(bf16)
+            send(RS_Z, k, rz_send.at[k], rz_recv.at[k], z_peers[k])
+
+    stages = (
+        (gather_column, 0), (gather_plane, 1), (first_products, 1), (reduce_chip, 4),
+        (hidden_grads, 2), (second_products, 3), (reduce_plane, 5),
+    )
+    for turn in range(planes + 5):
+        for stage, lag in stages:
+            if 0 <= turn - lag < planes:
+                stage(turn - lag)
+
+    total = pair[0, mine, :]
+    for k in range(1, planes):
+        arrived(RS_Z, k)
+        total = total + rz_recv[k].astype(f32)
+    out[...] = total[:, :feat].astype(bf16)
+    found = total[:, feat:]
+    result = jnp.zeros(ids.shape, f32)
+    slot = lax.broadcasted_iota(jnp.int32, ids.shape, 1)
+    for j in range(ids.shape[1]):
+        value = jnp.sum(jnp.where(lane == ids[:, j : j + 1], found, 0.0), axis=1, keepdims=True)
+        result = result + jnp.where(slot == j, value, 0.0)
+    out_gates[...] = result.astype(bf16)
+    for copy in copies.values():
+        copy.wait_send()
+
+
+def dense_on_device(tokens, grad_out, gates, expert_ids, w_gate, w_up, w_down):
+    planes = lax.axis_size("node") // 4
+    rows, feat = tokens.shape
+    hidden = w_gate.shape[2]
+    bf16, f32 = jnp.bfloat16, jnp.float32
+    wide = feat + LANES
+    vmem, hbm = pl.BlockSpec(memory_space=pltpu.VMEM), pl.BlockSpec(memory_space=pl.ANY)
+    return pl.pallas_call(
+        functools.partial(dense_kernel, planes),
+        out_shape=(
+            jax.ShapeDtypeStruct((rows, feat), bf16),
+            jax.ShapeDtypeStruct(expert_ids.shape, bf16),
+        ),
+        in_specs=[vmem] * 4 + [hbm] * 3,
+        out_specs=(vmem, vmem),
+        scratch_shapes=[
+            pltpu.VMEM((feat, hidden), bf16),
+            pltpu.VMEM((feat, hidden), bf16),
+            pltpu.VMEM((hidden, feat), bf16),
+            pltpu.VMEM((planes, 4 * rows, 2 * feat + LANES), bf16),
+            pltpu.VMEM((planes, 3, 4 * rows, hidden), f32),
+            pltpu.VMEM((planes, 3, 2 * rows, hidden), bf16),
+            pltpu.VMEM((planes, 3, 2 * rows, hidden), bf16),
+            pltpu.VMEM((planes, 4 * rows, 2 * hidden + LANES), bf16),
+            pltpu.VMEM((planes, 4 * rows, wide), f32),
+            pltpu.VMEM((planes, 2, rows, wide), bf16),
+            pltpu.VMEM((planes, 2, rows, wide), bf16),
+            pltpu.VMEM((planes, rows, wide), bf16),
+            pltpu.VMEM((planes, rows, wide), bf16),
+            pltpu.VMEM((planes, rows, wide), bf16),
+            pltpu.VMEM((planes, rows, wide), bf16),
+            pltpu.SemaphoreType.DMA((3,)),
+            pltpu.SemaphoreType.DMA((planes, KINDS)),
+            pltpu.SemaphoreType.DMA((planes, KINDS)),
+        ],
+        compiler_params=pltpu.CompilerParams(
+            collective_id=0, has_side_effects=True, vmem_limit_bytes=56 * 1024 * 1024
+        ),
+    )(tokens, grad_out, gates, expert_ids, w_gate, w_up, w_down)
 
 
 def local_grads(gate_pre, up_pre, back_pre, reduce_axis):
@@ -20,6 +271,9 @@
     tok_rows, feature_cols = tokens.shape
     top_count = expert_ids.shape[1]
     capacity = min(tok_rows, max(2, 2 * tok_rows * top_count // n_node))
+    planes = n_node // 4
+    if capacity == tok_rows and n_node == 4 * planes and planes & (planes - 1) == 0 and 3 * n_node <= LANES:
+        return dense_on_device(tokens, grad_out, gates, expert_ids, w_gate, w_up, w_down)
     flat_ids = expert_ids.reshape(-1)
     onehot = (flat_ids[:, None] == jnp.arange(n_node, dtype=jnp.int32)[None, :]).astype(jnp.int32)
     slot_rank = jnp.sum(onehot * (jnp.cumsum(onehot, axis=0) - 1), axis=1)

time: 194 us -> 72.2 us (0.37)
  blocking collectives: 76.1 us -> 0 us
  waiting for transfers between devices: 66.3 us -> 0 us
  Pallas kernels: 0 us -> 65.7 us
  between operations: 14.2 us -> 0.64 us
  matrix products: 12.8 us -> 0 us
  starting transfers between devices: 9.93 us -> 0 us
  other arithmetic: 6.78 us -> 0 us
    pallas_call x0 -> x1, Pallas kernels: none -> 65.7 us  [dense_on_device(): pl.pallas_call(functools.partial(dense_kernel, planes), out_shape=(jax.Sh...]
    all_to_all x1 -> x0, blocking collectives: 54.6 us -> none  [on_device(): lax.all_to_all(outgoing, 'node', split_axis=0, concat_axis=0, tiled=True)]
    reduce_scatter x1 -> x0, waiting for transfers between devices: 44 us -> none  [on_device(): lax.psum_scatter(jnp.concatenate([gate_pre, up_pre, back_pre], axis=1), '...]
    all_to_all x2 -> x0, waiting for transfers between devices: 22.3 us -> none  [the longest x1 20.5 us: on_device(): lax.all_to_all(sent_rows, 'node', split_axis=0, concat_axis=0, tiled=True)]
    all_gather x2 -> x0, blocking collectives: 16.5 us -> none  [the longest x1 8.7 us: on_device(): lax.all_gather(grad_up, 'local', axis=0, tiled=True)]
    dot_general x6 -> x0, matrix products: 12.8 us -> none  [the longest x1 4.51 us: on_device(): lax.dot_general(lax.all_gather(grad_gate, 'local', axis=0, tiled=True), g...]
    all_to_all x2 -> x0, starting transfers between devices: 9.89 us -> none  [the longest x1 5.69 us: on_device(): lax.all_to_all(sent_gates, 'node', split_axis=0, concat_axis=0, tiled=True)]
    psum x1 -> x0, blocking collectives: 4.92 us -> none  [on_device(): gate_total = lax.psum(partial_gate, 'local').astype(jnp.bfloat16)]
  transfers between devices with their start and end apart: 3 -> 0, of which waited for: 3 -> 0; matrix products, arithmetic and copies ran while one was open for 4% -> 0% of each run, Pallas kernels for 0% -> 0%
where the time goes in v1:
time: 72.2 us; the launch traced here: 71.9 us
  Pallas kernels  65.7 us (91%)
  local copies, waits for them, and re-layouts  5.51 us (8%)
    pallas_call x1, Pallas kernels, dense_on_device(): pl.pallas_call(functools.partial(dense_kernel, planes), out_shape=(jax.Sh...  65.7 us
    unnamed x3, local copies, waits for them, and re-layouts  4.18 us

profile of v1, /device:TPU:0, one launch (start us, length us, event | category | flops | bytes accessed | tf_op | source)
XLA Modules:
  0.0 71.9 jit_solution(12315527034359281219)
XLA Ops:
  0.6 1.4 %copy.9.gates = f32[16,8]{1,0:T(8,128)} copy(f32[16,8]{0,1:T(8,128)} %param.9) | data formatting | bytes 1024 | tf_op args[2]
  2.0 1.4 %copy.10.ids = s32[16,8]{1,0:T(8,128)} copy(s32[16,8]{0,1:T(8,128)} %param.10) | data formatting | bytes 1024 | tf_op args[3]
  3.3 65.7 %shard_map.86 = (bf16[16,2048]{1,0:T(8,128)(2,1)}, bf16[16,8]{1,0:T(8,128)(2,1)}) custom-call(bf16[16,2048]{1,0:T(8,128)(2,1)} %tokens.1, bf16[16,2048]{1,0:T(8,128)(2,1)} %grad_out.1, f32[16,8]{1,0:T(8,128)} %copy.9.gates, s32[16,8]{1,0:T(8,128)} %copy.10.ids, bf16[1,2048,1024]{2,1,0:T(8,128)(2,1)} %wg_hbm.1, bf16[1,2048,1024]{2,1,0:T(8,128)(2,1)} %wu_hbm.1, ...), custom_call_target="tpu_custom_call" | custom-call | tf_op jit(solution)/shard_map/pallas_call | solution.py:224
  69.1 1.3 %copy.11 = bf16[16,8]{0,1:T(8,128)(2,1)} copy(bf16[16,8]{1,0:T(8,128)(2,1)} %get-tuple-element.3) | data formatting | bytes 512 | tf_op jit(solution)/shard_map/pallas_call | solution.py:224
  70.4 1.5 %copy.13 = bf16[16,2048]{1,0:T(8,128)(2,1)} copy(bf16[16,2048]{1,0:T(8,128)(2,1)} %get-tuple-element.6) | data formatting | bytes 131072

commit v2 on v1

--- a/solution.py
+++ b/solution.py
@@ -24,7 +24,7 @@
 
 
 def dense_kernel(
-    planes, tokens, grad_out, gates, ids, wg_hbm, wu_hbm, wd_hbm, out, out_gates,
+    planes, tokens, grad_out, gates_t, ids_t, wg_hbm, wu_hbm, wd_hbm, out, out_gates,
     wg, wu, wd, gath, part, sum_send, sum_recv, grads, pair, rc_send, rc_recv,
     rx_send, rx_recv, rz_send, rz_recv, w_sem, send_sem, recv_sem,
 ):
@@ -46,8 +46,19 @@
     def block(x_, c_, size=rows):
         return pl.ds(pl.multiple_of((x_ * 2 + c_) * rows, rows), size)
 
-    mine, here = block(x, core), block(y, 0, half)
-    theirs = block(1 - y, 0, half)
+    mine = block(x, core)
+    chunks = [(0, x * half, half, 0)]
+    chunks += [(k, 0, 2 * half, 0) for k in range(1, planes)]
+    chunks += [(0, (1 - x) * half, half, rows)]
+    last = planes
+
+    def part_rows(chunk, which):
+        slot, base, size, place = chunks[chunk]
+        return pl.ds(pl.multiple_of(base + which * (size // 2), rows), size // 2)
+
+    def chunk_rows(chunk):
+        slot, base, size, place = chunks[chunk]
+        return pl.ds(base if isinstance(base, int) else pl.multiple_of(base, half), size)
 
     loads = [
         pltpu.make_async_copy(src.at[0], dst, w_sem.at[i])
@@ -66,8 +77,17 @@
     lane = lax.broadcasted_iota(jnp.int32, (rows, LANES), 1)
     expert_lane = lax.rem(lane, experts)
     weight = jnp.zeros((rows, LANES), f32)
-    for j in range(ids.shape[1]):
-        weight = weight + jnp.where(expert_lane == ids[:, j : j + 1], gates[:, j : j + 1], 0.0)
+    top_count = ids_t.shape[0]
+    diagonal = lax.broadcasted_iota(jnp.int32, (rows, rows), 0) == lax.broadcasted_iota(
+        jnp.int32, (rows, rows), 1
+    )
+
+    def column(line):
+        return jnp.sum(jnp.where(diagonal, line, 0.0), axis=1, keepdims=True)
+
+    ids = [column(ids_t[j : j + 1, :].astype(f32)).astype(jnp.int32) for j in range(top_count)]
+    for j in range(top_count):
+        weight = weight + jnp.where(expert_lane == ids[j], column(gates_t[j : j + 1, :]), 0.0)
     top = weight.astype(bf16).astype(f32)
     middle = (weight - top).astype(bf16).astype(f32)
     low = weight - top - middle
@@ -93,123 +113,185 @@
     def forward(kind, k, where, peer):
         send(kind, k, gath.at[k, where], gath.at[k, where], peer)
 
+    def gather_own():
+        forward(AG_A, 0, mine, sibling)
+        for k in range(1, planes):
+            send(AG_Z, k, gath.at[0, mine], gath.at[k, mine], z_peers[k])
+
     def gather_column(k):
         if k:
             arrived(AG_Z, k)
         forward(AG_X, k, mine, x_peer)
-        if k == 0:
-            for far in range(1, planes):
-                send(AG_Z, far, gath.at[0, mine], gath.at[far, mine], z_peers[far])
-        forward(AG_A, k, mine, sibling)
+        if k:
+            forward(AG_A, k, mine, sibling)
 
     def gather_plane(k):
         arrived(AG_X, k)
         forward(AG_B, k, block(1 - x, core), sibling)
 
-    def first_products(k):
-        arrived(AG_A, k)
-        arrived(AG_B, k)
+    def first_products(chunk, between=None):
+        slot, base, size, place = chunks[chunk]
+        where = chunk_rows(chunk)
+        if chunk < last:
+            arrived(AG_A, slot)
+        if chunk > 0:
+            arrived(AG_B, slot)
         for m in range(3):
-            if k == 0:
+            if chunk == 0:
                 loads[m].wait()
+            if m == 2 and between is not None:
+                between()
 
             def column_tile(j, carry, m=m):
                 at = pl.ds(pl.multiple_of(j * TILE, TILE), TILE)
                 if m < 2:
-                    value = jnp.dot(gath[k, :, :feat], (wg, wu)[m][:, at], preferred_element_type=f32)
+                    value = jnp.dot(
+                        gath[slot, where, :feat], (wg, wu)[m][:, at], preferred_element_type=f32
+                    )
                 else:
                     value = lax.dot_general(
-                        gath[k, :, feat : 2 * feat], wd[at, :], NT, preferred_element_type=f32
+                        gath[slot, where, feat : 2 * feat], wd[at, :], NT, preferred_element_type=f32
                     )
-                part[k, m, :, at] = value
+                part[slot, m, where, at] = value
                 return carry
 
             lax.fori_loop(0, hidden // TILE, column_tile, 0)
-            sum_send[k, m] = part[k, m, theirs, :].astype(bf16)
-            send(SUM_Y + m, k, sum_send.at[k, m], sum_recv.at[k, m], y_peer)
-
-    def hidden_grads(k):
+            box = pl.ds(place, size // 2)
+            sum_send[slot, m, box] = part[slot, m, part_rows(chunk, 1 - y), :].astype(bf16)
+            send(SUM_Y + m, chunk, sum_send.at[slot, m, box], sum_recv.at[slot, m, box], y_peer)
+
+    def hidden_grads(chunk):
+        slot, base, size, place = chunks[chunk]
+        here = part_rows(chunk, y)
         for m in range(3):
-            arrived(SUM_Y + m, k)
-        total = jnp.zeros((half, 1), f32)
+            arrived(SUM_Y + m, chunk)
+        total = jnp.zeros((size // 2, 1), f32)
         for j in range(hidden // TILE):
             at = pl.ds(j * TILE, TILE)
             gate, up, back = (
-                part[k, m, here, at] + sum_recv[k, m, :, at].astype(f32) for m in range(3)
+                part[slot, m, here, at]
+                + sum_recv[slot, m, place : place + size // 2, at].astype(f32)
+                for m in range(3)
             )
             sig = jax.nn.sigmoid(gate)
             act = gate * sig
             back_act = back * act
             total = total + jnp.sum(back_act * up, axis=1, keepdims=True)
-            grads[k, here, j * TILE : (j + 1) * TILE] = (
+            grads[slot, here, j * TILE : (j + 1) * TILE] = (
                 back * up * sig * (1.0 + gate * (1.0 - sig))
             ).astype(bf16)
-            grads[k, here, hidden + j * TILE : hidden + (j + 1) * TILE] = back_act.astype(bf16)
-        lanes = lax.broadcasted_iota(jnp.int32, (half, LANES), 1)
-        grads[k, here, 2 * hidden :] = jnp.where(lanes == node, total, 0.0).astype(bf16)
-        send(GRAD_Y, k, grads.at[k, here], grads.at[k, here], y_peer)
-
-    def second_products(k):
-        arrived(GRAD_Y, k)
-        lanes = lax.broadcasted_iota(jnp.int32, (2 * half, LANES), 1)
+            grads[slot, here, hidden + j * TILE : hidden + (j + 1) * TILE] = back_act.astype(bf16)
+        lanes = lax.broadcasted_iota(jnp.int32, (size // 2, LANES), 1)
+        grads[slot, here, 2 * hidden :] = jnp.where(lanes == node, total, 0.0).astype(bf16)
+        send(GRAD_Y, chunk, grads.at[slot, here], grads.at[slot, here], y_peer)
+
+    def second_products(chunk):
+        slot, base, size, place = chunks[chunk]
+        where = chunk_rows(chunk)
+        arrived(GRAD_Y, chunk)
+        lanes = lax.broadcasted_iota(jnp.int32, (size, LANES), 1)
         chosen = (lax.rem(lanes, experts) == node) & (lanes < 3 * experts)
         scale = jnp.sum(
-            jnp.where(chosen, gath[k, :, 2 * feat :].astype(f32), 0.0), axis=1, keepdims=True
+            jnp.where(chosen, gath[slot, where, 2 * feat :].astype(f32), 0.0), axis=1, keepdims=True
         )
 
         def feature_tile(j, carry):
             at = pl.ds(pl.multiple_of(j * TILE, TILE), TILE)
-            value = lax.dot_general(grads[k, :, :hidden], wg[at, :], NT, preferred_element_type=f32)
+            value = lax.dot_general(
+                grads[slot, where, :hidden], wg[at, :], NT, preferred_element_type=f32
+            )
             value = value + lax.dot_general(
-                grads[k, :, hidden : 2 * hidden], wu[at, :], NT, preferred_element_type=f32
+                grads[slot, where, hidden : 2 * hidden], wu[at, :], NT, preferred_element_type=f32
             )
-            pair[k, :, at] = value * scale
+            pair[slot, where, at] = value * scale
             return carry
 
         lax.fori_loop(0, feat // TILE, feature_tile, 0)
-        pair[k, :, feat:] = grads[k, :, 2 * hidden :].astype(f32)
-        for x_ in range(2):
-            rc_send[k, x_] = pair[k, block(x_, 1 - core), :].astype(bf16)
-        send(RS_C, k, rc_send.at[k], rc_recv.at[k], sibling)
-
-    def chip_sum(k, x_):
-        return pair[k, block(x_, core), :] + rc_recv[k, x_].astype(f32)
-
-    def reduce_chip(k):
-        arrived(RS_C, k)
-        rx_send[k] = chip_sum(k, 1 - x).astype(bf16)
-        send(RS_X, k, rx_send.at[k], rx_recv.at[k], x_peer)
+        pair[slot, where, feat:] = grads[slot, where, 2 * hidden :].astype(f32)
+        if chunk == 0:
+            rc_send[0, 0] = pair[0, block(x, 1 - core), :].astype(bf16)
+        elif chunk == last:
+            rc_send[0, 1] = pair[0, block(1 - x, 1 - core), :].astype(bf16)
+        else:
+            for x_ in range(2):
+                rc_send[slot, x_] = pair[slot, block(x_, 1 - core), :].astype(bf16)
+        if chunk in (0, last):
+            side = 0 if chunk == 0 else 1
+            send(RS_C, chunk, rc_send.at[0, side], rc_recv.at[0, side], sibling)
+        else:
+            send(RS_C, chunk, rc_send.at[slot], rc_recv.at[slot], sibling)
+
+    def reduce_chip(chunk):
+        slot = chunks[chunk][0]
+        arrived(RS_C, chunk)
+        other = rc_recv[0, 1] if chunk == last else rc_recv[slot, 1 - x]
+        rx_send[slot] = (pair[slot, block(1 - x, core), :] + other.astype(f32)).astype(bf16)
+        send(RS_X, slot, rx_send.at[slot], rx_recv.at[slot], x_peer)
 
     def reduce_plane(k):
         arrived(RS_X, k)
-        value = chip_sum(k, x) + rx_recv[k].astype(f32)
-        if k == 0:
-            pair[0, mine, :] = value
+        value = pair[k, mine, :] + rc_recv[k, x].astype(f32) + rx_recv[k].astype(f32)
+        rz_send[k] = value.astype(bf16)
+        send(RS_Z, k, rz_send.at[k], rz_recv.at[k], z_peers[k])
+
+    gather_own()
+    if planes > 1:
+        first_products(0, lambda: gather_column(1))
+    else:
+        first_products(0)
+    for k in range(1, planes):
+        gather_plane(k)
+        if k + 1 < planes:
+            first_products(k, lambda: gather_column(k + 1))
         else:
-            rz_send[k] = value.astype(bf16)
-            send(RS_Z, k, rz_send.at[k], rz_recv.at[k], z_peers[k])
-
-    stages = (
-        (gather_column, 0), (gather_plane, 1), (first_products, 1), (reduce_chip, 4),
-        (hidden_grads, 2), (second_products, 3), (reduce_plane, 5),
-    )
-    for turn in range(planes + 5):
-        for stage, lag in stages:
-            if 0 <= turn - lag < planes:
-                stage(turn - lag)
-
-    total = pair[0, mine, :]
+            gather_column(0)
+            first_products(k)
+        hidden_grads(k - 1)
+        if k >= 2:
+            second_products(k - 2)
+        if k >= 4:
+            reduce_chip(k - 3)
+        if k >= 5:
+            reduce_plane(k - 4)
+    if planes == 1:
+        gather_column(0)
+    gather_plane(0)
+    first_products(last)
+    hidden_grads(last - 1)
+    if planes >= 2:
+        second_products(last - 2)
+    if planes >= 4:
+        reduce_chip(last - 3)
+    if planes >= 5:
+        reduce_plane(last - 4)
+    hidden_grads(last)
+    if planes >= 3:
+        reduce_chip(last - 2)
+    if planes >= 4:
+        reduce_plane(last - 3)
+    second_products(last - 1)
+    if planes >= 3:
+        reduce_plane(last - 2)
+    if planes >= 2:
+        reduce_chip(last - 1)
+    second_products(last)
+    if planes >= 2:
+        reduce_plane(last - 1)
+    reduce_chip(last)
+
+    arrived(RS_C, 0)
+    total = pair[0, mine, :] + rc_recv[0, 0].astype(f32)
     for k in range(1, planes):
         arrived(RS_Z, k)
         total = total + rz_recv[k].astype(f32)
+    arrived(RS_X, 0)
+    total = total + rx_recv[0].astype(f32)
     out[...] = total[:, :feat].astype(bf16)
     found = total[:, feat:]
-    result = jnp.zeros(ids.shape, f32)
-    slot = lax.broadcasted_iota(jnp.int32, ids.shape, 1)
-    for j in range(ids.shape[1]):
-        value = jnp.sum(jnp.where(lane == ids[:, j : j + 1], found, 0.0), axis=1, keepdims=True)
-        result = result + jnp.where(slot == j, value, 0.0)
-    out_gates[...] = result.astype(bf16)
+    for j in range(top_count):
+        value = jnp.sum(jnp.where(lane == ids[j], found, 0.0), axis=1, keepdims=True)
+        line = jnp.sum(jnp.where(diagonal, value, 0.0), axis=0, keepdims=True)
+        out_gates[j : j + 1, :] = line.astype(bf16)
     for copy in copies.values():
         copy.wait_send()
 
@@ -221,11 +303,11 @@
     bf16, f32 = jnp.bfloat16, jnp.float32
     wide = feat + LANES
     vmem, hbm = pl.BlockSpec(memory_space=pltpu.VMEM), pl.BlockSpec(memory_space=pl.ANY)
-    return pl.pallas_call(
+    grad_tokens, grad_gates_t = pl.pallas_call(
         functools.partial(dense_kernel, planes),
         out_shape=(
             jax.ShapeDtypeStruct((rows, feat), bf16),
-            jax.ShapeDtypeStruct(expert_ids.shape, bf16),
+            jax.ShapeDtypeStruct(expert_ids.shape[::-1], bf16),
         ),
         in_specs=[vmem] * 4 + [hbm] * 3,
         out_specs=(vmem, vmem),
@@ -246,13 +328,14 @@
             pltpu.VMEM((planes, rows, wide), bf16),
             pltpu.VMEM((planes, rows, wide), bf16),
             pltpu.SemaphoreType.DMA((3,)),
-            pltpu.SemaphoreType.DMA((planes, KINDS)),
-            pltpu.SemaphoreType.DMA((planes, KINDS)),
+            pltpu.SemaphoreType.DMA((planes + 1, KINDS)),
+            pltpu.SemaphoreType.DMA((planes + 1, KINDS)),
         ],
         compiler_params=pltpu.CompilerParams(
             collective_id=0, has_side_effects=True, vmem_limit_bytes=56 * 1024 * 1024
         ),
-    )(tokens, grad_out, gates, expert_ids, w_gate, w_up, w_down)
+    )(tokens, grad_out, gates.T, expert_ids.T, w_gate, w_up, w_down)
+    return grad_tokens, grad_gates_t.T
 
 
 def local_grads(gate_pre, up_pre, back_pre, reduce_axis):

time: 72.2 us -> 75.2 us (1.042)
  Pallas kernels: 65.7 us -> 71.6 us
  local copies, waits for them, and re-layouts: 5.51 us -> 2.72 us
    pallas_call x1, Pallas kernels: 65.7 us -> 71.6 us  [dense_on_device(): pl.pallas_call(functools.partial(dense_kernel, planes), out_shape=(jax.Sh...]
    unnamed x3 -> x2, local copies, waits for them, and re-layouts: 4.18 us -> 2.72 us
    pallas_call x1 -> x0, local copies, waits for them, and re-layouts: 1.33 us -> none  [dense_on_device(): pl.pallas_call(functools.partial(dense_kernel, planes), out_shape=(jax.Sh...]
where the time goes in v2:
time: 75.2 us; the launch traced here: 74.9 us
  Pallas kernels  71.6 us (95%)
  local copies, waits for them, and re-layouts  2.72 us (4%)
    pallas_call x1, Pallas kernels, dense_on_device(): pl.pallas_call(functools.partial(dense_kernel, planes), out_shape=(jax.Sh...  71.6 us
    unnamed x2, local copies, waits for them, and re-layouts  2.72 us

profile of v2, /device:TPU:0, one launch (start us, length us, event | category | flops | bytes accessed | tf_op | source)
XLA Modules:
  0.0 74.9 jit_solution(12022742227749059540)
XLA Ops:
  0.6 71.6 %shard_map.86 = (bf16[16,2048]{1,0:T(8,128)(2,1)}, bf16[8,16]{1,0:T(8,128)(2,1)}) custom-call(bf16[16,2048]{1,0:T(8,128)(2,1)} %tokens.1, bf16[16,2048]{1,0:T(8,128)(2,1)} %grad_out.1, f32[8,16]{1,0:T(8,128)} %bitcast.3, s32[8,16]{1,0:T(8,128)} %bitcast.4, bf16[1,2048,1024]{2,1,0:T(8,128)(2,1)} %wg_hbm.1, bf16[1,2048,1024]{2,1,0:T(8,128)(2,1)} %wu_hbm.1, ...), custom_call_target="tpu_custom_call" | custom-call | tf_op jit(solution)/shard_map/pallas_call | solution.py:306
  72.2 1.5 %copy.11 = bf16[16,2048]{1,0:T(8,128)(2,1)} copy(bf16[16,2048]{1,0:T(8,128)(2,1)} %get-tuple-element.8) | data formatting | bytes 131072
  73.7 1.2 %copy.12 = bf16[16,8]{0,1:T(8,128)(2,1)} copy(bf16[16,8]{0,1:T(8,128)(2,1)} %bitcast.5) | data formatting | bytes 512

commit v3 on v0

--- a/solution.py
+++ b/solution.py
@@ -1,7 +1,309 @@
+import functools
+
 import jax
 import jax.numpy as jnp
 from jax import lax
+from jax.experimental import pallas as pl
+from jax.experimental.pallas import tpu as pltpu
 from jax.sharding import PartitionSpec as P
+
+MESH = pl.DeviceIdType.MESH
+LANES = 128
+TILE = 256
+NT = (((1,), (1,)), ((), ()))
+
+
+def flipped(value, bits):
+    place = 1
+    while place <= bits:
+        if bits & place:
+            value = value + place * (1 - 2 * lax.rem(lax.div(value, place), 2))
+        place *= 2
+    return value
+
+
+def dense_kernel(
+    planes, tokens, grad_out, gates_t, ids_t, wg_hbm, wu_hbm, wd_hbm, out, out_gates,
+    wg, wu, wd, gath, part, sum_send, sum_recv, grads, gate_sums, pair, rc_send, rc_recv,
+    rx_send, rx_recv, rz_send, rz_recv, w_sem, send_sem, recv_sem,
+):
+    node, y = lax.axis_index("node"), lax.axis_index("local")
+    core, x, z = lax.rem(node, 2), lax.rem(lax.div(node, 2), 2), lax.div(node, 4)
+    rows, feat = tokens.shape
+    hidden = wg.shape[1]
+    experts = 4 * planes
+    plane = 4 * rows
+    tiles = hidden // TILE
+    f32, bf16 = jnp.float32, jnp.bfloat16
+    halves = ((0, feat // 2), (feat // 2, feat + LANES))
+
+    def device(z_, x_, c_):
+        return (z_ * 4 + x_ * 2 + c_, y)
+
+    x_peer, sibling = device(z, 1 - x, core), device(z, x, 1 - core)
+    y_peer = (node, 1 - y)
+    z_peers = [None] + [device(flipped(z, k), x, core) for k in range(1, planes)]
+
+    def block(k, x_, c_):
+        return pl.ds(pl.multiple_of(k * plane + (x_ * 2 + c_) * rows, rows), rows)
+
+    def plane_rows(k):
+        return pl.ds(pl.multiple_of(k * plane, plane), plane)
+
+    mine = block(0, x, core)
+
+    loads = [
+        pltpu.make_async_copy(src.at[0], dst, w_sem.at[i])
+        for i, (src, dst) in enumerate(((wg_hbm, wg), (wu_hbm, wu), (wd_hbm, wd)))
+    ]
+    for load in loads:
+        load.start()
+
+    barrier = pltpu.get_barrier_semaphore()
+    peers = [x_peer, sibling, y_peer] + z_peers[1:]
+    for peer in peers:
+        pl.semaphore_signal(barrier, inc=1, device_id=peer, device_id_type=MESH)
+
+    gath[mine, :feat] = tokens[...]
+    gath[mine, feat : 2 * feat] = grad_out[...]
+    lane = lax.broadcasted_iota(jnp.int32, (rows, LANES), 1)
+    expert_lane = lax.rem(lane, experts)
+    weight = jnp.zeros((rows, LANES), f32)
+    top_count = ids_t.shape[0]
+    diagonal = lax.broadcasted_iota(jnp.int32, (rows, rows), 0) == lax.broadcasted_iota(
+        jnp.int32, (rows, rows), 1
+    )
+
+    def column(line):
+        return jnp.sum(jnp.where(diagonal, line, 0.0), axis=1, keepdims=True)
+
+    ids = [column(ids_t[j : j + 1, :].astype(f32)).astype(jnp.int32) for j in range(top_count)]
+    for j in range(top_count):
+        weight = weight + jnp.where(expert_lane == ids[j], column(gates_t[j : j + 1, :]), 0.0)
+    top = weight.astype(bf16).astype(f32)
+    middle = (weight - top).astype(bf16).astype(f32)
+    low = weight - top - middle
+    packed = jnp.where(
+        lane < experts, top, jnp.where(lane < 2 * experts, middle, jnp.where(lane < 3 * experts, low, 0.0))
+    )
+    gath[mine, 2 * feat :] = packed.astype(bf16)
+
+    pl.semaphore_wait(barrier, len(peers))
+
+    copies = {}
+
+    def send(name, src, dst, peer):
+        i = len(copies)
+        copies[name] = pltpu.make_async_remote_copy(
+            src_ref=src, dst_ref=dst, send_sem=send_sem.at[i], recv_sem=recv_sem.at[i],
+            device_id=peer, device_id_type=MESH,
+        )
+        copies[name].start()
+
+    def arrived(*name):
+        copies[name].wait_recv()
+
+    def forward(name, where, peer):
+        send(name, gath.at[where], gath.at[where], peer)
+
+    def gather_own():
+        forward(("x", 0), mine, x_peer)
+        for k in range(1, planes):
+            send(("z", k), gath.at[mine], gath.at[block(k, x, core)], z_peers[k])
+        forward(("a", 0), mine, sibling)
+
+    def gather_column(k):
+        arrived("z", k)
+        forward(("x", k), block(k, x, core), x_peer)
+        forward(("a", k), block(k, x, core), sibling)
+
+    def gather_plane(k):
+        arrived("x", k)
+        forward(("b", k), block(k, 1 - x, core), sibling)
+
+    def first_products(ch, j):
+        where, at = pl.ds(ch * 2 * plane, 2 * plane), pl.ds(j * TILE, TILE)
+        if j == 0:
+            for k in (2 * ch, 2 * ch + 1):
+                arrived("a", k)
+                arrived("b", k)
+        for m in range(3):
+            if ch == 0 and j == 0:
+                loads[m].wait()
+            if m < 2:
+                value = jnp.dot(gath[where, :feat], (wg, wu)[m][:, at], preferred_element_type=f32)
+            else:
+                value = lax.dot_general(
+                    gath[where, feat : 2 * feat], wd[at, :], NT, preferred_element_type=f32
+                )
+            part[m, where, at] = value
+            sum_send[ch, j, m] = part[m, plane_rows(2 * ch + 1 - y), at].astype(bf16)
+        send(("sum", ch, j), sum_send.at[ch, j], sum_recv.at[ch, j], y_peer)
+
+    gate_totals = {}
+
+    def hidden_grads(ch, j):
+        here, at = plane_rows(2 * ch + y), pl.ds(j * TILE, TILE)
+        arrived("sum", ch, j)
+        gate, up, back = (part[m, here, at] + sum_recv[ch, j, m].astype(f32) for m in range(3))
+        sig = jax.nn.sigmoid(gate)
+        act = gate * sig
+        back_act = back * act
+        total = jnp.sum(back_act * up, axis=1, keepdims=True)
+        gate_totals[ch] = gate_totals[ch] + total if j else total
+        grads[j, here, :TILE] = (back * up * sig * (1.0 + gate * (1.0 - sig))).astype(bf16)
+        grads[j, here, TILE:] = back_act.astype(bf16)
+        send(("grad", ch, j), grads.at[j, here], grads.at[j, here], y_peer)
+        if j == tiles - 1:
+            lanes = lax.broadcasted_iota(jnp.int32, (plane, LANES), 1)
+            gate_sums[here] = jnp.where(lanes == node, gate_totals[ch], 0.0).astype(bf16)
+            send(("gates", ch), gate_sums.at[here], gate_sums.at[here], y_peer)
+
+    def second_products(ch, h):
+        where = pl.ds(ch * 2 * plane, 2 * plane)
+        if h == 0:
+            for j in range(tiles):
+                arrived("grad", ch, j)
+        lanes = lax.broadcasted_iota(jnp.int32, (2 * plane, LANES), 1)
+        chosen = (lax.rem(lanes, experts) == node) & (lanes < 3 * experts)
+        scale = jnp.sum(
+            jnp.where(chosen, gath[where, 2 * feat :].astype(f32), 0.0), axis=1, keepdims=True
+        )
+
+        def feature_tile(i, carry):
+            at = pl.ds(pl.multiple_of(i * TILE, TILE), TILE)
+            value = jnp.zeros((2 * plane, TILE), f32)
+            for j in range(tiles):
+                for m in range(2):
+                    value = value + lax.dot_general(
+                        grads[j, where, m * TILE : (m + 1) * TILE],
+                        (wg, wu)[m][at, j * TILE : (j + 1) * TILE],
+                        NT,
+                        preferred_element_type=f32,
+                    )
+            pair[where, at] = value * scale
+            return carry
+
+        lax.fori_loop(h * feat // 2 // TILE, (h + 1) * feat // 2 // TILE, feature_tile, 0)
+        if h == 1:
+            arrived("gates", ch)
+            pair[where, feat:] = gate_sums[where].astype(f32)
+        lo, hi = halves[h]
+        for k in (2 * ch, 2 * ch + 1):
+            for x_ in range(2):
+                rc_send[k, x_, :, lo:hi] = pair[block(k, x_, 1 - core), lo:hi].astype(bf16)
+        box = (pl.ds(2 * ch, 2), slice(None), slice(None), pl.ds(lo, hi - lo))
+        send(("core", ch, h), rc_send.at[box], rc_recv.at[box], sibling)
+
+    def reduce_chip(ch, h):
+        lo, hi = halves[h]
+        arrived("core", ch, h)
+        for k in (2 * ch, 2 * ch + 1):
+            value = pair[block(k, 1 - x, core), lo:hi] + rc_recv[k, 1 - x, :, lo:hi].astype(f32)
+            rx_send[k, :, lo:hi] = value.astype(bf16)
+        box = (pl.ds(2 * ch, 2), slice(None), pl.ds(lo, hi - lo))
+        send(("across", ch, h), rx_send.at[box], rx_recv.at[box], x_peer)
+
+    def reduce_plane(ch, h):
+        lo, hi = halves[h]
+        arrived("across", ch, h)
+        for k in (2 * ch, 2 * ch + 1):
+            value = pair[block(k, x, core), lo:hi] + rc_recv[k, x, :, lo:hi].astype(f32)
+            value = value + rx_recv[k, :, lo:hi].astype(f32)
+            if k == 0:
+                pair[mine, lo:hi] = value
+            else:
+                rz_send[k, :, lo:hi] = value.astype(bf16)
+                box = (k, slice(None), pl.ds(lo, hi - lo))
+                send(("home", k, h), rz_send.at[box], rz_recv.at[box], z_peers[k])
+
+    count = planes // 2
+    gather_own()
+    gather_column(1)
+    gather_plane(0)
+    gather_plane(1)
+    for ch in range(count):
+        ahead = []
+        if ch + 1 < count:
+            k = 2 * ch + 2
+            ahead = [(gather_column, k), (gather_column, k + 1), (gather_plane, k), (gather_plane, k + 1)]
+        for j in range(tiles):
+            first_products(ch, j)
+            if j < len(ahead):
+                ahead[j][0](ahead[j][1])
+            if ch:
+                hidden_grads(ch - 1, j)
+        for stage, k in ahead[tiles:]:
+            stage(k)
+    for j in range(tiles):
+        hidden_grads(count - 1, j)
+    for ch in range(count + 1):
+        for h in range(2):
+            if ch < count:
+                second_products(ch, h)
+            if ch:
+                reduce_chip(ch - 1, h)
+        if ch:
+            for h in range(2):
+                reduce_plane(ch - 1, h)
+
+    found = None
+    for h, (lo, hi) in enumerate(halves):
+        total = pair[mine, lo:hi]
+        for k in range(1, planes):
+            arrived("home", k, h)
+            total = total + rz_recv[k, :, lo:hi].astype(f32)
+        out[:, lo : min(hi, feat)] = total[:, : min(hi, feat) - lo].astype(bf16)
+        found = total[:, hi - lo - LANES :]
+    for j in range(top_count):
+        value = jnp.sum(jnp.where(lane == ids[j], found, 0.0), axis=1, keepdims=True)
+        line = jnp.sum(jnp.where(diagonal, value, 0.0), axis=0, keepdims=True)
+        out_gates[j : j + 1, :] = line.astype(bf16)
+    for copy in copies.values():
+        copy.wait_send()
+
+
+def dense_on_device(tokens, grad_out, gates, expert_ids, w_gate, w_up, w_down):
+    planes = lax.axis_size("node") // 4
+    rows, feat = tokens.shape
+    hidden = w_gate.shape[2]
+    bf16, f32 = jnp.bfloat16, jnp.float32
+    wide, tiles = feat + LANES, hidden // TILE
+    vmem, hbm = pl.BlockSpec(memory_space=pltpu.VMEM), pl.BlockSpec(memory_space=pl.ANY)
+    grad_tokens, grad_gates_t = pl.pallas_call(
+        functools.partial(dense_kernel, planes),
+        out_shape=(
+            jax.ShapeDtypeStruct((rows, feat), bf16),
+            jax.ShapeDtypeStruct(expert_ids.shape[::-1], bf16),
+        ),
+        in_specs=[vmem] * 4 + [hbm] * 3,
+        out_specs=(vmem, vmem),
+        scratch_shapes=[
+            pltpu.VMEM((feat, hidden), bf16),
+            pltpu.VMEM((feat, hidden), bf16),
+            pltpu.VMEM((hidden, feat), bf16),
+            pltpu.VMEM((planes * 4 * rows, 2 * feat + LANES), bf16),
+            pltpu.VMEM((3, planes * 4 * rows, hidden), f32),
+            pltpu.VMEM((planes // 2, tiles, 3, 4 * rows, TILE), bf16),
+            pltpu.VMEM((planes // 2, tiles, 3, 4 * rows, TILE), bf16),
+            pltpu.VMEM((tiles, planes * 4 * rows, 2 * TILE), bf16),
+            pltpu.VMEM((planes * 4 * rows, LANES), bf16),
+            pltpu.VMEM((planes * 4 * rows, wide), f32),
+            pltpu.VMEM((planes, 2, rows, wide), bf16),
+            pltpu.VMEM((planes, 2, rows, wide), bf16),
+            pltpu.VMEM((planes, rows, wide), bf16),
+            pltpu.VMEM((planes, rows, wide), bf16),
+            pltpu.VMEM((planes, rows, wide), bf16),
+            pltpu.VMEM((planes, rows, wide), bf16),
+            pltpu.SemaphoreType.DMA((3,)),
+            pltpu.SemaphoreType.DMA((planes * (8 + tiles),)),
+            pltpu.SemaphoreType.DMA((planes * (8 + tiles),)),
+        ],
+        compiler_params=pltpu.CompilerParams(
+            collective_id=0, has_side_effects=True, vmem_limit_bytes=56 * 1024 * 1024
+        ),
+    )(tokens, grad_out, gates.T, expert_ids.T, w_gate, w_up, w_down)
+    return grad_tokens, grad_gates_t.T
 
 
 def local_grads(gate_pre, up_pre, back_pre, reduce_axis):
@@ -20,6 +322,9 @@
     tok_rows, feature_cols = tokens.shape
     top_count = expert_ids.shape[1]
     capacity = min(tok_rows, max(2, 2 * tok_rows * top_count // n_node))
+    planes = n_node // 4
+    if capacity == tok_rows and n_node == 4 * planes and planes > 1 and planes & (planes - 1) == 0 and 3 * n_node <= LANES:
+        return dense_on_device(tokens, grad_out, gates, expert_ids, w_gate, w_up, w_down)
     flat_ids = expert_ids.reshape(-1)
     onehot = (flat_ids[:, None] == jnp.arange(n_node, dtype=jnp.int32)[None, :]).astype(jnp.int32)
     slot_rank = jnp.sum(onehot * (jnp.cumsum(onehot, axis=0) - 1), axis=1)

time: 194 us -> 71.4 us (0.37)
  blocking collectives: 76.1 us -> 0 us
  Pallas kernels: 0 us -> 67.8 us
  waiting for transfers between devices: 66.3 us -> 0 us
  between operations: 14.2 us -> 0.64 us
  matrix products: 12.8 us -> 0 us
  starting transfers between devices: 9.93 us -> 0 us
  other arithmetic: 6.78 us -> 0 us
  local copies, waits for them, and re-layouts: 6.59 us -> 2.72 us
    pallas_call x0 -> x1, Pallas kernels: none -> 67.8 us  [dense_on_device(): pl.pallas_call(functools.partial(dense_kernel, planes), out_shape=(jax.Sh...]
    all_to_all x1 -> x0, blocking collectives: 54.6 us -> none  [on_device(): lax.all_to_all(outgoing, 'node', split_axis=0, concat_axis=0, tiled=True)]
    reduce_scatter x1 -> x0, waiting for transfers between devices: 44 us -> none  [on_device(): lax.psum_scatter(jnp.concatenate([gate_pre, up_pre, back_pre], axis=1), '...]
    all_to_all x2 -> x0, waiting for transfers between devices: 22.3 us -> none  [the longest x1 20.5 us: on_device(): lax.all_to_all(sent_rows, 'node', split_axis=0, concat_axis=0, tiled=True)]
    all_gather x2 -> x0, blocking collectives: 16.5 us -> none  [the longest x1 8.7 us: on_device(): lax.all_gather(grad_up, 'local', axis=0, tiled=True)]
    dot_general x6 -> x0, matrix products: 12.8 us -> none  [the longest x1 4.51 us: on_device(): lax.dot_general(lax.all_gather(grad_gate, 'local', axis=0, tiled=True), g...]
    all_to_all x2 -> x0, starting transfers between devices: 9.89 us -> none  [the longest x1 5.69 us: on_device(): lax.all_to_all(sent_gates, 'node', split_axis=0, concat_axis=0, tiled=True)]
    psum x1 -> x0, blocking collectives: 4.92 us -> none  [on_device(): gate_total = lax.psum(partial_gate, 'local').astype(jnp.bfloat16)]
  transfers between devices with their start and end apart: 3 -> 0, of which waited for: 3 -> 0; matrix products, arithmetic and copies ran while one was open for 4% -> 0% of each run, Pallas kernels for 0% -> 0%
where the time goes in v3:
time: 71.4 us; the launch traced here: 71.2 us
  Pallas kernels  67.8 us (95%)
  local copies, waits for them, and re-layouts  2.72 us (4%)
    pallas_call x1, Pallas kernels, dense_on_device(): pl.pallas_call(functools.partial(dense_kernel, planes), out_shape=(jax.Sh...  67.8 us
    unnamed x2, local copies, waits for them, and re-layouts  2.72 us

profile of v3, /device:TPU:0, one launch (start us, length us, event | category | flops | bytes accessed | tf_op | source)
XLA Modules:
  0.0 71.2 jit_solution(13566157445932312903)
XLA Ops:
  0.6 67.8 %shard_map.86 = (bf16[16,2048]{1,0:T(8,128)(2,1)}, bf16[8,16]{1,0:T(8,128)(2,1)}) custom-call(bf16[16,2048]{1,0:T(8,128)(2,1)} %tokens.1, bf16[16,2048]{1,0:T(8,128)(2,1)} %grad_out.1, f32[8,16]{1,0:T(8,128)} %bitcast.3, s32[8,16]{1,0:T(8,128)} %bitcast.4, bf16[1,2048,1024]{2,1,0:T(8,128)(2,1)} %wg_hbm.1, bf16[1,2048,1024]{2,1,0:T(8,128)(2,1)} %wu_hbm.1, ...), custom_call_target="tpu_custom_call" | custom-call | tf_op jit(solution)/shard_map/pallas_call | solution.py:273
  68.4 1.5 %copy.11 = bf16[16,2048]{1,0:T(8,128)(2,1)} copy(bf16[16,2048]{1,0:T(8,128)(2,1)} %get-tuple-element.8) | data formatting | bytes 131072
  69.9 1.2 %copy.12 = bf16[16,8]{0,1:T(8,128)(2,1)} copy(bf16[16,8]{0,1:T(8,128)(2,1)} %bitcast.5) | data formatting | bytes 512

commit v4 on v3

--- a/solution.py
+++ b/solution.py
@@ -47,10 +47,22 @@
     def block(k, x_, c_):
         return pl.ds(pl.multiple_of(k * plane + (x_ * 2 + c_) * rows, rows), rows)
 
-    def plane_rows(k):
-        return pl.ds(pl.multiple_of(k * plane, plane), plane)
-
     mine = block(0, x, core)
+    chunks = [(0, 1)] + ([(1, 1)] if planes > 2 else []) + [(planes // 2, planes - planes // 2)]
+    last = len(chunks) - 1
+
+    def chunk_planes(ch):
+        return range(chunks[ch][0], chunks[ch][0] + chunks[ch][1])
+
+    def chunk_rows(ch):
+        return pl.ds(chunks[ch][0] * plane, chunks[ch][1] * plane)
+
+    def part_rows(ch, which):
+        size = chunks[ch][1] * plane // 2
+        return pl.ds(pl.multiple_of(chunks[ch][0] * plane + which * size, 2 * rows), size)
+
+    def part_box(ch):
+        return pl.ds(chunks[ch][0] * plane // 2, chunks[ch][1] * plane // 2)
 
     loads = [
         pltpu.make_async_copy(src.at[0], dst, w_sem.at[i])
@@ -106,10 +118,12 @@
     def forward(name, where, peer):
         send(name, gath.at[where], gath.at[where], peer)
 
+    def send_far(k):
+        send(("z", k), gath.at[mine], gath.at[block(k, x, core)], z_peers[k])
+
     def gather_own():
         forward(("x", 0), mine, x_peer)
-        for k in range(1, planes):
-            send(("z", k), gath.at[mine], gath.at[block(k, x, core)], z_peers[k])
+        send_far(1)
         forward(("a", 0), mine, sibling)
 
     def gather_column(k):
@@ -122,9 +136,9 @@
         forward(("b", k), block(k, 1 - x, core), sibling)
 
     def first_products(ch, j):
-        where, at = pl.ds(ch * 2 * plane, 2 * plane), pl.ds(j * TILE, TILE)
+        where, at, box = chunk_rows(ch), pl.ds(j * TILE, TILE), part_box(ch)
         if j == 0:
-            for k in (2 * ch, 2 * ch + 1):
+            for k in chunk_planes(ch):
                 arrived("a", k)
                 arrived("b", k)
         for m in range(3):
@@ -137,15 +151,16 @@
                     gath[where, feat : 2 * feat], wd[at, :], NT, preferred_element_type=f32
                 )
             part[m, where, at] = value
-            sum_send[ch, j, m] = part[m, plane_rows(2 * ch + 1 - y), at].astype(bf16)
-        send(("sum", ch, j), sum_send.at[ch, j], sum_recv.at[ch, j], y_peer)
+            sum_send[j, m, box] = part[m, part_rows(ch, 1 - y), at].astype(bf16)
+        box = (j, slice(None), box)
+        send(("sum", ch, j), sum_send.at[box], sum_recv.at[box], y_peer)
 
     gate_totals = {}
 
     def hidden_grads(ch, j):
-        here, at = plane_rows(2 * ch + y), pl.ds(j * TILE, TILE)
+        here, at, box = part_rows(ch, y), pl.ds(j * TILE, TILE), part_box(ch)
         arrived("sum", ch, j)
-        gate, up, back = (part[m, here, at] + sum_recv[ch, j, m].astype(f32) for m in range(3))
+        gate, up, back = (part[m, here, at] + sum_recv[j, m, box].astype(f32) for m in range(3))
         sig = jax.nn.sigmoid(gate)
         act = gate * sig
         back_act = back * act
@@ -155,25 +170,24 @@
         grads[j, here, TILE:] = back_act.astype(bf16)
         send(("grad", ch, j), grads.at[j, here], grads.at[j, here], y_peer)
         if j == tiles - 1:
-            lanes = lax.broadcasted_iota(jnp.int32, (plane, LANES), 1)
+            lanes = lax.broadcasted_iota(jnp.int32, (chunks[ch][1] * plane // 2, LANES), 1)
             gate_sums[here] = jnp.where(lanes == node, gate_totals[ch], 0.0).astype(bf16)
             send(("gates", ch), gate_sums.at[here], gate_sums.at[here], y_peer)
 
-    def second_products(ch, h):
-        where = pl.ds(ch * 2 * plane, 2 * plane)
-        if h == 0:
-            for j in range(tiles):
-                arrived("grad", ch, j)
-        lanes = lax.broadcasted_iota(jnp.int32, (2 * plane, LANES), 1)
-        chosen = (lax.rem(lanes, experts) == node) & (lanes < 3 * experts)
-        scale = jnp.sum(
-            jnp.where(chosen, gath[where, 2 * feat :].astype(f32), 0.0), axis=1, keepdims=True
-        )
+    def second_products(ch, picked, features):
+        where, size = chunk_rows(ch), chunks[ch][1] * plane
+        scale = None
+        if picked[-1] == tiles - 1:
+            lanes = lax.broadcasted_iota(jnp.int32, (size, LANES), 1)
+            chosen = (lax.rem(lanes, experts) == node) & (lanes < 3 * experts)
+            scale = jnp.sum(
+                jnp.where(chosen, gath[where, 2 * feat :].astype(f32), 0.0), axis=1, keepdims=True
+            )
 
         def feature_tile(i, carry):
             at = pl.ds(pl.multiple_of(i * TILE, TILE), TILE)
-            value = jnp.zeros((2 * plane, TILE), f32)
-            for j in range(tiles):
+            value = pair[where, at] if picked[0] else jnp.zeros((size, TILE), f32)
+            for j in picked:
                 for m in range(2):
                     value = value + lax.dot_general(
                         grads[j, where, m * TILE : (m + 1) * TILE],
@@ -181,33 +195,45 @@
                         NT,
                         preferred_element_type=f32,
                     )
-            pair[where, at] = value * scale
+            pair[where, at] = value if scale is None else value * scale
             return carry
 
-        lax.fori_loop(h * feat // 2 // TILE, (h + 1) * feat // 2 // TILE, feature_tile, 0)
+        lax.fori_loop(features[0] // TILE, features[1] // TILE, feature_tile, 0)
+
+    def early_products(ch, j):
+        arrived("grad", ch, j)
+        second_products(ch, [j], (0, feat))
+
+    def late_products(ch, h):
+        where = chunk_rows(ch)
+        picked = [tiles - 1] if ch == last else list(range(tiles))
+        if h == 0:
+            for j in picked:
+                arrived("grad", ch, j)
+        second_products(ch, picked, (h * feat // 2, (h + 1) * feat // 2))
         if h == 1:
             arrived("gates", ch)
             pair[where, feat:] = gate_sums[where].astype(f32)
         lo, hi = halves[h]
-        for k in (2 * ch, 2 * ch + 1):
+        for k in chunk_planes(ch):
             for x_ in range(2):
                 rc_send[k, x_, :, lo:hi] = pair[block(k, x_, 1 - core), lo:hi].astype(bf16)
-        box = (pl.ds(2 * ch, 2), slice(None), slice(None), pl.ds(lo, hi - lo))
+        box = (pl.ds(*chunks[ch]), slice(None), slice(None), pl.ds(lo, hi - lo))
         send(("core", ch, h), rc_send.at[box], rc_recv.at[box], sibling)
 
     def reduce_chip(ch, h):
         lo, hi = halves[h]
         arrived("core", ch, h)
-        for k in (2 * ch, 2 * ch + 1):
+        for k in chunk_planes(ch):
             value = pair[block(k, 1 - x, core), lo:hi] + rc_recv[k, 1 - x, :, lo:hi].astype(f32)
             rx_send[k, :, lo:hi] = value.astype(bf16)
-        box = (pl.ds(2 * ch, 2), slice(None), pl.ds(lo, hi - lo))
+        box = (pl.ds(*chunks[ch]), slice(None), pl.ds(lo, hi - lo))
         send(("across", ch, h), rx_send.at[box], rx_recv.at[box], x_peer)
 
     def reduce_plane(ch, h):
         lo, hi = halves[h]
         arrived("across", ch, h)
-        for k in (2 * ch, 2 * ch + 1):
+        for k in chunk_planes(ch):
             value = pair[block(k, x, core), lo:hi] + rc_recv[k, x, :, lo:hi].astype(f32)
             value = value + rx_recv[k, :, lo:hi].astype(f32)
             if k == 0:
@@ -217,35 +243,46 @@
                 box = (k, slice(None), pl.ds(lo, hi - lo))
                 send(("home", k, h), rz_send.at[box], rz_recv.at[box], z_peers[k])
 
-    count = planes // 2
+    def both(stage, ch):
+        for h in range(2):
+            stage(ch, h)
+
     gather_own()
+    gather_plane(0)
     gather_column(1)
-    gather_plane(0)
-    gather_plane(1)
-    for ch in range(count):
+    for k in range(2, planes):
+        send_far(k)
+    for ch in range(last + 1):
         ahead = []
-        if ch + 1 < count:
-            k = 2 * ch + 2
-            ahead = [(gather_column, k), (gather_column, k + 1), (gather_plane, k), (gather_plane, k + 1)]
+        if ch == 0 and last > 0:
+            ahead = [(gather_plane, 1)]
+        elif ch < last:
+            ahead = [(gather_column, k) for k in chunk_planes(last)]
+            ahead += [(gather_plane, k) for k in chunk_planes(last)]
         for j in range(tiles):
             first_products(ch, j)
-            if j < len(ahead):
-                ahead[j][0](ahead[j][1])
+            for stage, k in ahead[j : j + 1]:
+                stage(k)
             if ch:
                 hidden_grads(ch - 1, j)
         for stage, k in ahead[tiles:]:
             stage(k)
+    pending = [(ch, h) for ch in range(last) for h in range(2)]
     for j in range(tiles):
-        hidden_grads(count - 1, j)
-    for ch in range(count + 1):
-        for h in range(2):
-            if ch < count:
-                second_products(ch, h)
-            if ch:
-                reduce_chip(ch - 1, h)
-        if ch:
-            for h in range(2):
-                reduce_plane(ch - 1, h)
+        hidden_grads(last, j)
+        for ch, h in pending[j : j + 1]:
+            late_products(ch, h)
+    for ch, h in pending[tiles:]:
+        late_products(ch, h)
+    for j in range(tiles - 1):
+        early_products(last, j)
+        if j < last:
+            both(reduce_chip, j)
+        if 1 <= j <= last:
+            both(reduce_plane, j - 1)
+    both(late_products, last)
+    both(reduce_chip, last)
+    both(reduce_plane, last)
 
     found = None
     for h, (lo, hi) in enumerate(halves):
@@ -284,8 +321,8 @@
             pltpu.VMEM((hidden, feat), bf16),
             pltpu.VMEM((planes * 4 * rows, 2 * feat + LANES), bf16),
             pltpu.VMEM((3, planes * 4 * rows, hidden), f32),
-            pltpu.VMEM((planes // 2, tiles, 3, 4 * rows, TILE), bf16),
-            pltpu.VMEM((planes // 2, tiles, 3, 4 * rows, TILE), bf16),
+            pltpu.VMEM((tiles, 3, planes * 2 * rows, TILE), bf16),
+            pltpu.VMEM((tiles, 3, planes * 2 * rows, TILE), bf16),
             pltpu.VMEM((tiles, planes * 4 * rows, 2 * TILE), bf16),
             pltpu.VMEM((planes * 4 * rows, LANES), bf16),
             pltpu.VMEM((planes * 4 * rows, wide), f32),
@@ -296,8 +333,8 @@
             pltpu.VMEM((planes, rows, wide), bf16),
             pltpu.VMEM((planes, rows, wide), bf16),
             pltpu.SemaphoreType.DMA((3,)),
-            pltpu.SemaphoreType.DMA((planes * (8 + tiles),)),
-            pltpu.SemaphoreType.DMA((planes * (8 + tiles),)),
+            pltpu.SemaphoreType.DMA((planes * (12 + tiles),)),
+            pltpu.SemaphoreType.DMA((planes * (12 + tiles),)),
         ],
         compiler_params=pltpu.CompilerParams(
             collective_id=0, has_side_effects=True, vmem_limit_bytes=56 * 1024 * 1024

time: 71.4 us -> 73.5 us (1.029)
  Pallas kernels: 67.8 us -> 69.9 us
    pallas_call x1, Pallas kernels: 67.8 us -> 69.9 us  [dense_on_device(): pl.pallas_call(functools.partial(dense_kernel, planes), out_shape=(jax.Sh...]
where the time goes in v4:
time: 73.5 us; the launch traced here: 73.2 us
  Pallas kernels  69.9 us (95%)
  local copies, waits for them, and re-layouts  2.72 us (4%)
    pallas_call x1, Pallas kernels, dense_on_device(): pl.pallas_call(functools.partial(dense_kernel, planes), out_shape=(jax.Sh...  69.9 us
    unnamed x2, local copies, waits for them, and re-layouts  2.72 us

profile of v4, /device:TPU:0, one launch (start us, length us, event | category | flops | bytes accessed | tf_op | source)
XLA Modules:
  0.0 73.2 jit_solution(11492678121956346711)
XLA Ops:
  0.6 69.9 %shard_map.86 = (bf16[16,2048]{1,0:T(8,128)(2,1)}, bf16[8,16]{1,0:T(8,128)(2,1)}) custom-call(bf16[16,2048]{1,0:T(8,128)(2,1)} %tokens.1, bf16[16,2048]{1,0:T(8,128)(2,1)} %grad_out.1, f32[8,16]{1,0:T(8,128)} %bitcast.3, s32[8,16]{1,0:T(8,128)} %bitcast.4, bf16[1,2048,1024]{2,1,0:T(8,128)(2,1)} %wg_hbm.1, bf16[1,2048,1024]{2,1,0:T(8,128)(2,1)} %wu_hbm.1, ...), custom_call_target="tpu_custom_call" | custom-call | tf_op jit(solution)/shard_map/pallas_call | solution.py:310
  70.5 1.5 %copy.11 = bf16[16,2048]{1,0:T(8,128)(2,1)} copy(bf16[16,2048]{1,0:T(8,128)(2,1)} %get-tuple-element.8) | data formatting | bytes 131072
  72.0 1.2 %copy.12 = bf16[16,8]{0,1:T(8,128)(2,1)} copy(bf16[16,8]{0,1:T(8,128)(2,1)} %bitcast.5) | data formatting | bytes 512

commit v5 on v4

--- a/solution.py
+++ b/solution.py
@@ -123,8 +123,9 @@
 
     def gather_own():
         forward(("x", 0), mine, x_peer)
-        send_far(1)
         forward(("a", 0), mine, sibling)
+        for k in range(1, planes):
+            send_far(k)
 
     def gather_column(k):
         arrived("z", k)
@@ -249,24 +250,17 @@
 
     gather_own()
     gather_plane(0)
-    gather_column(1)
-    for k in range(2, planes):
-        send_far(k)
+    ahead = [[] for unused in range(tiles * (last + 1))]
+    for k in range(1, planes):
+        ahead[min(2 * k - 2 if k < 3 else k, tiles * last - 2)].append((gather_column, k))
+        ahead[min(1 if k == 1 else 2 * k, tiles * last - 1)].append((gather_plane, k))
     for ch in range(last + 1):
-        ahead = []
-        if ch == 0 and last > 0:
-            ahead = [(gather_plane, 1)]
-        elif ch < last:
-            ahead = [(gather_column, k) for k in chunk_planes(last)]
-            ahead += [(gather_plane, k) for k in chunk_planes(last)]
         for j in range(tiles):
             first_products(ch, j)
-            for stage, k in ahead[j : j + 1]:
+            for stage, k in ahead[ch * tiles + j]:
                 stage(k)
             if ch:
                 hidden_grads(ch - 1, j)
-        for stage, k in ahead[tiles:]:
-            stage(k)
     pending = [(ch, h) for ch in range(last) for h in range(2)]
     for j in range(tiles):
         hidden_grads(last, j)

time: 73.5 us -> 73.1 us (level)
  no operation moved by 1% of the time
where the time goes in v5:
time: 73.1 us; the launch traced here: 72.9 us
  Pallas kernels  69.5 us (95%)
  local copies, waits for them, and re-layouts  2.72 us (4%)
    pallas_call x1, Pallas kernels, dense_on_device(): pl.pallas_call(functools.partial(dense_kernel, planes), out_shape=(jax.Sh...  69.5 us
    unnamed x2, local copies, waits for them, and re-layouts  2.72 us

profile of v5, /device:TPU:0, one launch (start us, length us, event | category | flops | bytes accessed | tf_op | source)
XLA Modules:
  0.0 72.9 jit_solution(3474629906903682041)
XLA Ops:
  0.6 69.5 %shard_map.86 = (bf16[16,2048]{1,0:T(8,128)(2,1)}, bf16[8,16]{1,0:T(8,128)(2,1)}) custom-call(bf16[16,2048]{1,0:T(8,128)(2,1)} %tokens.1, bf16[16,2048]{1,0:T(8,128)(2,1)} %grad_out.1, f32[8,16]{1,0:T(8,128)} %bitcast.3, s32[8,16]{1,0:T(8,128)} %bitcast.4, bf16[1,2048,1024]{2,1,0:T(8,128)(2,1)} %wg_hbm.1, bf16[1,2048,1024]{2,1,0:T(8,128)(2,1)} %wu_hbm.1, ...), custom_call_target="tpu_custom_call" | custom-call | tf_op jit(solution)/shard_map/pallas_call | solution.py:304
  70.2 1.5 %copy.11 = bf16[16,2048]{1,0:T(8,128)(2,1)} copy(bf16[16,2048]{1,0:T(8,128)(2,1)} %get-tuple-element.8) | data formatting | bytes 131072
  71.7 1.2 %copy.12 = bf16[16,8]{0,1:T(8,128)(2,1)} copy(bf16[16,8]{0,1:T(8,128)(2,1)} %bitcast.5) | data formatting | bytes 512

commit v6 on v1

--- a/solution.py
+++ b/solution.py
@@ -24,7 +24,7 @@
 
 
 def dense_kernel(
-    planes, tokens, grad_out, gates, ids, wg_hbm, wu_hbm, wd_hbm, out, out_gates,
+    planes, tokens, grad_out, gates_t, ids_t, wg_hbm, wu_hbm, wd_hbm, out, out_gates,
     wg, wu, wd, gath, part, sum_send, sum_recv, grads, pair, rc_send, rc_recv,
     rx_send, rx_recv, rz_send, rz_recv, w_sem, send_sem, recv_sem,
 ):
@@ -66,8 +66,17 @@
     lane = lax.broadcasted_iota(jnp.int32, (rows, LANES), 1)
     expert_lane = lax.rem(lane, experts)
     weight = jnp.zeros((rows, LANES), f32)
-    for j in range(ids.shape[1]):
-        weight = weight + jnp.where(expert_lane == ids[:, j : j + 1], gates[:, j : j + 1], 0.0)
+    top_count = ids_t.shape[0]
+    diagonal = lax.broadcasted_iota(jnp.int32, (rows, rows), 0) == lax.broadcasted_iota(
+        jnp.int32, (rows, rows), 1
+    )
+
+    def column(line):
+        return jnp.sum(jnp.where(diagonal, line, 0.0), axis=1, keepdims=True)
+
+    ids = [column(ids_t[j : j + 1, :].astype(f32)).astype(jnp.int32) for j in range(top_count)]
+    for j in range(top_count):
+        weight = weight + jnp.where(expert_lane == ids[j], column(gates_t[j : j + 1, :]), 0.0)
     top = weight.astype(bf16).astype(f32)
     middle = (weight - top).astype(bf16).astype(f32)
     low = weight - top - middle
@@ -204,12 +213,10 @@
         total = total + rz_recv[k].astype(f32)
     out[...] = total[:, :feat].astype(bf16)
     found = total[:, feat:]
-    result = jnp.zeros(ids.shape, f32)
-    slot = lax.broadcasted_iota(jnp.int32, ids.shape, 1)
-    for j in range(ids.shape[1]):
-        value = jnp.sum(jnp.where(lane == ids[:, j : j + 1], found, 0.0), axis=1, keepdims=True)
-        result = result + jnp.where(slot == j, value, 0.0)
-    out_gates[...] = result.astype(bf16)
+    for j in range(top_count):
+        value = jnp.sum(jnp.where(lane == ids[j], found, 0.0), axis=1, keepdims=True)
+        line = jnp.sum(jnp.where(diagonal, value, 0.0), axis=0, keepdims=True)
+        out_gates[j : j + 1, :] = line.astype(bf16)
     for copy in copies.values():
         copy.wait_send()
 
@@ -221,11 +228,11 @@
     bf16, f32 = jnp.bfloat16, jnp.float32
     wide = feat + LANES
     vmem, hbm = pl.BlockSpec(memory_space=pltpu.VMEM), pl.BlockSpec(memory_space=pl.ANY)
-    return pl.pallas_call(
+    grad_tokens, grad_gates_t = pl.pallas_call(
         functools.partial(dense_kernel, planes),
         out_shape=(
             jax.ShapeDtypeStruct((rows, feat), bf16),
-            jax.ShapeDtypeStruct(expert_ids.shape, bf16),
+            jax.ShapeDtypeStruct(expert_ids.shape[::-1], bf16),
         ),
         in_specs=[vmem] * 4 + [hbm] * 3,
         out_specs=(vmem, vmem),
@@ -252,7 +259,8 @@
         compiler_params=pltpu.CompilerParams(
             collective_id=0, has_side_effects=True, vmem_limit_bytes=56 * 1024 * 1024
         ),
-    )(tokens, grad_out, gates, expert_ids, w_gate, w_up, w_down)
+    )(tokens, grad_out, gates.T, expert_ids.T, w_gate, w_up, w_down)
+    return grad_tokens, grad_gates_t.T
 
 
 def local_grads(gate_pre, up_pre, back_pre, reduce_axis):

time: 72.2 us -> 69 us (0.956)
  local copies, waits for them, and re-layouts: 5.51 us -> 2.72 us
    unnamed x3 -> x2, local copies, waits for them, and re-layouts: 4.18 us -> 2.72 us
    pallas_call x1 -> x0, local copies, waits for them, and re-layouts: 1.33 us -> none  [dense_on_device(): pl.pallas_call(functools.partial(dense_kernel, planes), out_shape=(jax.Sh...]
where the time goes in v6:
time: 69 us; the launch traced here: 68.8 us
  Pallas kernels  65.4 us (95%)
  local copies, waits for them, and re-layouts  2.72 us (4%)
    pallas_call x1, Pallas kernels, dense_on_device(): pl.pallas_call(functools.partial(dense_kernel, planes), out_shape=(jax.Sh...  65.4 us
    unnamed x2, local copies, waits for them, and re-layouts  2.72 us

profile of v6, /device:TPU:0, one launch (start us, length us, event | category | flops | bytes accessed | tf_op | source)
XLA Modules:
  0.0 68.8 jit_solution(4697292580494680507)
XLA Ops:
  0.6 65.4 %shard_map.86 = (bf16[16,2048]{1,0:T(8,128)(2,1)}, bf16[8,16]{1,0:T(8,128)(2,1)}) custom-call(bf16[16,2048]{1,0:T(8,128)(2,1)} %tokens.1, bf16[16,2048]{1,0:T(8,128)(2,1)} %grad_out.1, f32[8,16]{1,0:T(8,128)} %bitcast.3, s32[8,16]{1,0:T(8,128)} %bitcast.4, bf16[1,2048,1024]{2,1,0:T(8,128)(2,1)} %wg_hbm.1, bf16[1,2048,1024]{2,1,0:T(8,128)(2,1)} %wu_hbm.1, ...), custom_call_target="tpu_custom_call" | custom-call | tf_op jit(solution)/shard_map/pallas_call | solution.py:231
  66.1 1.5 %copy.11 = bf16[16,2048]{1,0:T(8,128)(2,1)} copy(bf16[16,2048]{1,0:T(8,128)(2,1)} %get-tuple-element.8) | data formatting | bytes 131072
  67.6 1.2 %copy.12 = bf16[16,8]{0,1:T(8,128)(2,1)} copy(bf16[16,8]{0,1:T(8,128)(2,1)} %bitcast.5) | data formatting | bytes 512

commit v7 on v6

--- a/solution.py
+++ b/solution.py
@@ -9,7 +9,7 @@
 
 MESH = pl.DeviceIdType.MESH
 LANES = 128
-TILE = 256
+TILE = 512
 AG_Z, AG_X, AG_A, AG_B, SUM_Y, GRAD_Y, RS_C, RS_X, RS_Z, KINDS = 0, 1, 2, 3, 4, 7, 8, 9, 10, 11
 NT = (((1,), (1,)), ((), ()))
 

time: 69 us -> 65.5 us (0.949)
  Pallas kernels: 65.4 us -> 61.9 us
    pallas_call x1, Pallas kernels: 65.4 us -> 61.9 us  [dense_on_device(): pl.pallas_call(functools.partial(dense_kernel, planes), out_shape=(jax.Sh...]
where the time goes in v7:
time: 65.5 us; the launch traced here: 65.3 us
  Pallas kernels  61.9 us (95%)
  local copies, waits for them, and re-layouts  2.72 us (4%)
    pallas_call x1, Pallas kernels, dense_on_device(): pl.pallas_call(functools.partial(dense_kernel, planes), out_shape=(jax.Sh...  61.9 us
    unnamed x2, local copies, waits for them, and re-layouts  2.72 us

profile of v7, /device:TPU:0, one launch (start us, length us, event | category | flops | bytes accessed | tf_op | source)
XLA Modules:
  0.0 65.3 jit_solution(12778399146163898786)
XLA Ops:
  0.6 61.9 %shard_map.86 = (bf16[16,2048]{1,0:T(8,128)(2,1)}, bf16[8,16]{1,0:T(8,128)(2,1)}) custom-call(bf16[16,2048]{1,0:T(8,128)(2,1)} %tokens.1, bf16[16,2048]{1,0:T(8,128)(2,1)} %grad_out.1, f32[8,16]{1,0:T(8,128)} %bitcast.3, s32[8,16]{1,0:T(8,128)} %bitcast.4, bf16[1,2048,1024]{2,1,0:T(8,128)(2,1)} %wg_hbm.1, bf16[1,2048,1024]{2,1,0:T(8,128)(2,1)} %wu_hbm.1, ...), custom_call_target="tpu_custom_call" | custom-call | tf_op jit(solution)/shard_map/pallas_call | solution.py:231
  62.5 1.5 %copy.11 = bf16[16,2048]{1,0:T(8,128)(2,1)} copy(bf16[16,2048]{1,0:T(8,128)(2,1)} %get-tuple-element.8) | data formatting | bytes 131072
  64.0 1.2 %copy.12 = bf16[16,8]{0,1:T(8,128)(2,1)} copy(bf16[16,8]{0,1:T(8,128)(2,1)} %bitcast.5) | data formatting | bytes 512
